TPU v7x, 256 devices: a whole 4x4x8 slice. The times are simulated.
256 devices in a mesh: pair: 8 (over y, x_lo), zone: 32 (over x_hi, z, core).
Axes of the slice: x: 4 (x_hi: 2, x_lo: 2; x = x_hi * 2 + x_lo), y: 4, z: 8, core: 2. Of those that a mesh axis runs over, the one named last changes fastest.
Arguments:
- vel_a: bfloat16 [64, 2, 3, 57344], P('pair', None, None, 'zone'), may hold values from -4.1875 to 4.1875
- vel_b: bfloat16 [256, 2, 3, 57344], P('pair', None, None, 'zone'), may hold values from -4.1875 to 4.1875
- panel_modes: bfloat16 [200, 57344], P(None, 'zone'), may hold values from -0.0234375 to 0.0234375
- modal_stress: bfloat16 [200, 16384], P(None, 'zone'), may hold values from -0.4375 to 0.4375
- freq_a: float32 [64], P('pair'), may hold values from 0.3 to 1.5
- freq_b: float32 [256], replicated, may hold values from 0.3 to 1.5
- mode_freq: float32 [200], replicated, may hold values from 0.6 to 3
- damping: float32 [200], replicated, may hold values from 0.05 to 0.2
Outputs:
- stress: bfloat16 [16384, 2, 64, 256], P('zone', None, 'pair')
All inputs are finite; a program needn't handle non-finite values.
Results may differ from a plain program's by a relative error of at most 0.0058.
Values may be sent and summed in bfloat16 or wider, within the bound.
A program may use at most 64 MiB of HBM per device.

v0:
```python
import jax
import jax.numpy as jnp
from jax import lax
from jax.sharding import PartitionSpec as P


def quadratic(first_vel, second_vel):
    pressure_re = jnp.zeros(
        (first_vel.shape[0], second_vel.shape[0], first_vel.shape[3]), jnp.float32
    )
    pressure_im = jnp.zeros(
        (first_vel.shape[0], second_vel.shape[0], first_vel.shape[3]), jnp.float32
    )
    for component in range(3):
        first_re = first_vel[:, None, 0, component]
        first_im = first_vel[:, None, 1, component]
        second_re = second_vel[None, :, 0, component]
        second_im = second_vel[None, :, 1, component]
        pressure_re = pressure_re + first_re * second_re - first_im * second_im
        pressure_im = pressure_im + first_re * second_im + first_im * second_re
    return jnp.stack([-0.5 * pressure_re, -0.5 * pressure_im]).astype(jnp.bfloat16)


def respond_flat(sum_freq, forces, mode_freq, damping):
    mode_square = (mode_freq * mode_freq)[:, None]
    detuning = mode_square - sum_freq[None] * sum_freq[None]
    damping_term = (2.0 * damping * mode_freq)[:, None] * sum_freq[None]
    denominator = detuning * detuning + damping_term * damping_term
    recept_re = mode_square * detuning / denominator
    recept_im = -mode_square * damping_term / denominator
    response_re = recept_re * forces[:, 0] - recept_im * forces[:, 1]
    response_im = recept_re * forces[:, 1] + recept_im * forces[:, 0]
    return jnp.stack([response_re, response_im], axis=1).astype(jnp.bfloat16)


def recover(modal_stress, response):
    return jnp.einsum(
        "me,mrc->erc", modal_stress, response, preferred_element_type=jnp.float32
    ).astype(jnp.bfloat16)


def local(vel_a, vel_b, panel_modes, modal_stress, freq_a, freq_b, mode_freq, damping):
    modes_count = panel_modes.shape[0]
    first_count = vel_a.shape[0]
    second_count = freq_b.shape[0]
    first_vel = vel_a.astype(jnp.float32)
    pressure = quadratic(
        first_vel, lax.all_gather(vel_b, "pair", axis=0, tiled=True).astype(jnp.float32)
    )
    forces = jnp.einsum("mk,rabk->mrab", panel_modes, pressure, preferred_element_type=jnp.float32)
    partial_forces = forces
    flat_count = first_count * second_count
    flat_forces = partial_forces.reshape(modes_count, 2, flat_count)
    sum_freq = (freq_a[:, None] + freq_b[None, :]).reshape(flat_count)
    element_count = modal_stress.shape[1]
    forces = lax.psum(flat_forces, "zone")
    response = respond_flat(sum_freq, forces, mode_freq, damping)
    stress = recover(modal_stress, response)
    return stress.reshape(element_count, 2, first_count, second_count)


def solution(mesh):
    in_specs = (
        P("pair", None, None, "zone"),
        P("pair", None, None, "zone"),
        P(None, "zone"),
        P(None, "zone"),
        P("pair"),
        P(),
        P(),
        P(),
    )
    out_specs = P("zone", None, "pair", None)
    return jax.shard_map(local, mesh=mesh, in_specs=in_specs, out_specs=out_specs, check_vma=False)
```

profile of v0, /device:TPU:1, one launch (start us, length us, event | category | flops | bytes accessed | tf_op | source)
XLA Modules:
  0.0 453.2 jit_solution(9547213363928652718)
XLA Ops:
  6.5 0.0 copy-start
  6.5 0.0 all-gather.2.cloned.1.call-start
  6.5 2.1 copy.11
  8.6 0.0 all-gather.2.cloned.1.call-update
  8.6 0.0 all-reduce.2.cloned.1.call-start
  8.7 0.9 copy_convert_fusion
  9.7 120.5 %all-gather.2.cloned.1.call-done = bf16[256,2,3,1792]{3,0,2,1:T(8,128)(2,1)} async-done(((bf16[32,2,3,1792]{3,0,2,1:T(8,128)(2,1)}), bf16[256,2,3,1792]{3,0,2,1:T(8,128)(2,1)}) %all-gather.2.cloned.1.call-update) | async-done | bytes 5505040 | tf_op jit(solution)/shard_map/all_gather | solution.py:48
  130.2 3.5 convert_element_type.15
  133.7 4.3 slice_bitcast_fusion.5
  138.1 13.8 %multiply_convert_fusion.1 = (bf16[1,8,256,1792]{3,2,1,0:T(8,128)(2,1)S(1)}, bf16[1,8,256,1792]{3,2,1,0:T(8,128)(2,1)S(1)}) fusion(f32[256,1792]{1,0:T(8,128)} %get-tuple-element.8, f32[8,1792]{1,0:T(8,128)S(1)} %get-tuple-element.16, f32[256,1792]{1,0:T(8,128)} %get-tuple-element.9, f32[8,1792]{1,0:T(8,128)S(1)} %get-tuple-element.17, ...), kind=kLoop, calls=%fused_computation.5 | loop fusion | flops 95420416 | bytes 26034176 | tf_op jit(solution)/shard_map/convert.2
  151.9 0.0 copy-done
  151.9 5.3 %fusion.4 = f32[2,8,25,8,256]{4,3,2,1,0:T(8,128)S(1)} fusion(bf16[1,8,256,1792]{3,2,1,0:T(8,128)(2,1)S(1)} %get-tuple-element.6, bf16[1,8,256,1792]{3,2,1,0:T(8,128)(2,1)S(1)} %get-tuple-element.5, bf16[200,1792]{1,0:T(8,128)(2,1)S(1)} %copy-done), kind=kOutput, calls=%fused_computation.11 | convolution fusion | flops 2943352832 | bytes 18673664 | tf_op jit(solution)/shard_map/mk,rabk->mrab/dot_general | solution.py:50
  157.2 0.0 copy-start.1
  157.2 0.0 copy-start.4
  157.2 0.0 copy-start.2
  157.2 0.0 copy-start.3
  157.2 2.1 copy.15
  159.3 0.0 copy-start.5
  159.3 0.0 all-reduce.2.cloned.1.call-update
  159.4 0.0 copy-done.1
  159.4 0.0 copy-done.4
  159.4 0.1 add_bitcast_fusion
  159.5 0.0 copy-done.2
  159.5 0.0 copy-done.3
  159.5 272.7 %all-reduce.2.cloned.1.call-done = f32[200,2,2048]{2,0,1:T(8,128)} async-done(((f32[200,2,2048]{2,0,1:T(8,128)}), f32[200,2,2048]{2,0,1:T(8,128)}) %all-reduce.2.cloned.1.call-update) | async-done | bytes 3276816 | tf_op jit(solution)/shard_map/psum | solution.py:56
  432.2 3.0 subtract_convert_fusion
  435.2 0.0 copy-done.5
  435.2 3.4 convolution_convert_fusion
  438.6 7.8 %copy.13 = bf16[512,2,8,256]{3,2,1,0:T(8,128)(2,1)} copy(bf16[512,2,8,256]{0,3,2,1:T(8,128)(2,1)} %bitcast.43) | data formatting | bytes 8388608 | tf_op jit(solution)/shard_map/reshape | solution.py:59
  (4 shorter events, 0.0 us)
Async XLA Ops:
  6.5 145.4 %copy-start = (bf16[200,1792]{1,0:T(8,128)(2,1)S(1)}, bf16[200,1792]{1,0:T(8,128)(2,1)}, u32[]{:S(2)}) copy-start(bf16[200,1792]{1,0:T(8,128)(2,1)} %param.10) | copy-start | bytes 2150404
  6.5 123.6 %all-gather.2.cloned.1.call-start = ((), (), s32[]{:S(2)}) async-start(), calls=%async_computation | async-start | bytes 6193152 | tf_op jit(solution)/shard_map/all_gather | solution.py:48
  8.6 423.5 %all-reduce.2.cloned.1.call-start = ((), (), s32[]{:S(2)}) async-start(), calls=%async_computation.1 | async-start | bytes 6553600 | tf_op jit(solution)/shard_map/psum | solution.py:56
  157.2 2.2 copy-start.1
  157.2 2.2 copy-start.4
  157.2 2.3 copy-start.2
  157.2 2.3 copy-start.3
  159.3 275.9 %copy-start.5 = (bf16[200,512]{1,0:T(8,128)(2,1)S(1)}, bf16[200,512]{1,0:T(8,128)(2,1)}, u32[]{:S(2)}) copy-start(bf16[200,512]{1,0:T(8,128)(2,1)} %param.11) | copy-start | bytes 614404
Sparse Core Ops, SparseCore 0:
  9.2 120.9 all-gather.1
  159.5 272.6 all-reduce.1
where the time goes:
time: 456 us; the launch traced here: 453 us
  waiting for transfers between devices  393 us (86%)
  other arithmetic  21.4 us (5%)
  local copies, waits for them, and re-layouts  16.4 us (4%)
  between operations  13.5 us (3%)
  matrix products  8.62 us (2%)
    psum x1, waiting for transfers between devices, local(): forces = lax.psum(flat_forces, 'zone')  273 us
    all_gather x1, waiting for transfers between devices, local(): lax.all_gather(vel_b, 'pair', axis=0, tiled=True).astype(jnp.float32)  120 us
    another operation x2, other arithmetic  16.9 us
  transfers between devices with their start and end apart: 2, of which 2 were waited for; matrix products, arithmetic and copies ran while one was open for 0% of the time, Pallas kernels for 0%

commit v1 on v0

v1 whole, which is shorter than its diff:
```python
import functools

import jax
import jax.numpy as jnp
from jax import lax
from jax.experimental import pallas as pl
from jax.experimental.pallas import tpu as pltpu
from jax.sharding import PartitionSpec as P

MESH = pl.DeviceIdType.MESH
F32 = jnp.float32
BF16 = jnp.bfloat16

A8 = 8
B32 = 32
KD = 1792
KT = KD // 128
M = 200
MH = 104
STEPS = ("plus", "minus")


def main_kernel(
    va, vb, modes, fa, fbt, msq, mdf,
    r_out,
    vel, fas, vf, uf, prs, grid_f, tx_sib, rx_sib, tx_z, rx_z, tx_x, rx_x, resp,
    vel_ss, vel_rs, fa_ss, fa_rs, sib_ss, sib_rs, z_ss, z_rs, x_ss, x_rs,
    a_ss, a_rs, g_ss, g_rs, gs_ss, gs_rs, loc_sem,
):
    pair = lax.axis_index("pair")
    zone = lax.axis_index("zone")
    y, xl = pair // 2, pair % 2
    core, z, xh = zone % 2, (zone // 2) % 8, zone // 16

    def dev(dy=0, dx=0, dz=0, dh=0, dc=0):
        return (
            ((y + dy) % 4) * 2 + (xl + dx) % 2,
            (((xh + dh) % 2) * 8 + (z + dz + 8) % 8) * 2 + (core + dc) % 2,
        )

    def exchange_peer(yq):
        return (yq * 2 + core, (xh * 8 + z) * 2 + xl)

    cross = xl != core

    barrier = pltpu.get_barrier_semaphore()
    pair_peers = [(dy, dx) for dy in range(4) for dx in range(2) if (dy, dx) != (0, 0)]
    for dy, dx in pair_peers:
        pl.semaphore_signal(barrier, inc=1, device_id=dev(dy=dy, dx=dx), device_id_type=MESH)
    for kw in (dict(dc=1), dict(dz=1), dict(dz=-1), dict(dh=1)):
        pl.semaphore_signal(barrier, inc=1, device_id=dev(**kw), device_id_type=MESH)

    @pl.when(cross)
    def _():
        for yq in range(4):
            pl.semaphore_signal(barrier, inc=1, device_id=exchange_peer(yq), device_id_type=MESH)

    pl.semaphore_wait(barrier, 11 + 4 * ((xl + core) % 2))

    def vel_copy(src, dst, k, to, half=None):
        s = vel.at[src] if half is None else vel.at[src, :, pl.ds(half, KD // 2)]
        d = vel.at[dst] if half is None else vel.at[dst, :, pl.ds(half, KD // 2)]
        return pltpu.make_async_remote_copy(
            src_ref=s, dst_ref=d, send_sem=vel_ss.at[k], recv_sem=vel_rs.at[k],
            device_id=to, device_id_type=MESH)

    own_vel = pltpu.make_async_copy(va, vel.at[0], loc_sem.at[0])
    own_vel.start()
    own_fa = pltpu.make_async_copy(fa, fas.at[0], loc_sem.at[1])
    own_fa.start()
    own_vel.wait()
    own_fa.wait()
    c_x = vel_copy(0, 1, 0, dev(dx=1))
    c_yp = vel_copy(0, 6, 1, dev(dy=1))
    c_ym = vel_copy(0, 2, 2, dev(dy=3))
    c_xyp = vel_copy(1, 7, 3, dev(dy=1))
    c_xym = vel_copy(1, 3, 4, dev(dy=3))
    c_fyp = vel_copy(6, 4, 5, dev(dy=1), 0)
    c_fym = vel_copy(2, 4, 6, dev(dy=3), KD // 2)
    c_x2 = vel_copy(4, 5, 7, dev(dx=1))
    c_x.start()
    c_yp.start()
    c_ym.start()
    fa_copies = []
    for n, (dy, dx) in enumerate(pair_peers):
        slot = 2 * ((4 - dy) % 4) + dx
        cp = pltpu.make_async_remote_copy(
            src_ref=fas.at[0], dst_ref=fas.at[slot], send_sem=fa_ss.at[n], recv_sem=fa_rs.at[n],
            device_id=dev(dy=dy, dx=dx), device_id_type=MESH)
        cp.start()
        fa_copies.append(cp)

    def zero_pad(n, _):
        grid_f[n // 4, 4 + n % 4, 96:104, :] = jnp.zeros((8, 128), F32)
        tx_sib[n // 4, 4 + n % 4, 96:104, :] = jnp.zeros((8, 128), BF16)
        return 0

    lax.fori_loop(0, 16, zero_pad, 0)

    def prep(kt, _):
        lanes = pl.ds(pl.multiple_of(kt * 128, 128), 128)
        for c in range(3):
            vr = vb[c * 64:c * 64 + 32, lanes].astype(F32)
            vi = vb[c * 64 + 32:c * 64 + 64, lanes].astype(F32)
            vf[kt, c * 3] = vr
            vf[kt, c * 3 + 1] = vi - vr
            vf[kt, c * 3 + 2] = vr + vi
        return 0

    lax.fori_loop(0, KT, prep, 0)

    def sib_copy(j):
        return pltpu.make_async_remote_copy(
            src_ref=tx_sib.at[j], dst_ref=rx_sib.at[j], send_sem=sib_ss.at[j], recv_sem=sib_rs.at[j],
            device_id=dev(dc=1), device_id_type=MESH)

    def block(i, _):
        j, dx = i // 2, i % 2
        dy = j + (j // 2) * (5 - 2 * j)
        slot = 2 * dy + dx

        @pl.when(i == 1)
        def _():
            c_x.wait_recv()
            c_xyp.start()
            c_xym.start()

        @pl.when(i == 2)
        def _():
            c_yp.wait_recv()
            c_fyp.start()
            c_ym.wait_recv()
            c_fym.start()

        @pl.when(i == 3)
        def _():
            c_xym.wait_recv()

        @pl.when(i == 5)
        def _():
            c_xyp.wait_recv()
            c_fyp.wait_recv()
            c_fym.wait_recv()
            c_x2.start()

        @pl.when(i == 7)
        def _():
            c_x2.wait_recv()

        def tile(kt, _):
            lanes = pl.ds(pl.multiple_of(kt * 128, 128), 128)
            for c in range(3):
                both = vel[slot, c * 16:c * 16 + 16, lanes].astype(F32)
                ur, ui = both[0:8] * -0.5, both[8:16] * -0.5
                uf[c * 24:c * 24 + 8] = ur
                uf[c * 24 + 8:c * 24 + 16] = ui
                uf[c * 24 + 16:c * 24 + 24] = ur + ui
            for a in range(A8):
                row = (a // 2) * 128 + (a % 2) * 32
                for half in range(2):
                    b = slice(half * 16, half * 16 + 16)
                    k1 = k2 = k3 = None
                    for c in range(3):
                        ur = uf[c * 24 + a:c * 24 + a + 1, :]
                        ui = uf[c * 24 + 8 + a:c * 24 + 8 + a + 1, :]
                        us = uf[c * 24 + 16 + a:c * 24 + 16 + a + 1, :]
                        t1 = vf[kt, c * 3, b, :] * us
                        t2 = vf[kt, c * 3 + 1, b, :] * ur
                        t3 = vf[kt, c * 3 + 2, b, :] * ui
                        k1 = t1 if k1 is None else k1 + t1
                        k2 = t2 if k2 is None else k2 + t2
                        k3 = t3 if k3 is None else k3 + t3
                    prs[row + half * 16:row + half * 16 + 16, lanes] = (k1 - k3).astype(BF16)
                    prs[row + 64 + half * 16:row + 64 + half * 16 + 16, lanes] = (k1 + k2).astype(BF16)
            return 0

        lax.fori_loop(0, KT, tile, 0)
        mine = (xl + dx) % 2 == core

        for zl in range(4):
            f = lax.dot_general(
                modes[...], prs[zl * 128:zl * 128 + 128, :], (((1,), (1,)), ((), ())),
                preferred_element_type=F32)

            @pl.when(mine)
            def _():
                grid_f[j, zl] = f[0:104]
                grid_f[j, 4 + zl, 0:96] = f[104:200]

            @pl.when(jnp.logical_not(mine))
            def _():
                tx_sib[j, zl] = f[0:104].astype(BF16)
                tx_sib[j, 4 + zl, 0:96] = f[104:200].astype(BF16)

        @pl.when(jnp.logical_not(mine))
        def _():
            sib_copy(j).start()

        return 0

    lax.fori_loop(0, 8, block, 0)

    for cp in (c_x, c_yp, c_ym, c_xyp, c_xym, c_fyp, c_fym, c_x2):
        cp.wait_send()

    def add_sibling(j, _):
        sib_copy(j).wait_recv()

        def add(t, _):
            grid_f[j, t] = grid_f[j, t] + rx_sib[j, t].astype(F32)
            return 0

        lax.fori_loop(0, 8, add, 0)
        return 0

    lax.fori_loop(0, 4, add_sibling, 0)

    def z_copy(d, s, j):
        return pltpu.make_async_remote_copy(
            src_ref=tx_z.at[d, s, j], dst_ref=rx_z.at[d, s, j],
            send_sem=z_ss.at[d, s, j], recv_sem=z_rs.at[d, s, j],
            device_id=dev(dz=1 if d == 0 else -1), device_id_type=MESH)

    for s in range(4):
        for j in range(4):
            for d in range(2):
                first = 0 if j % 2 == d else 1
                if s < first:
                    continue
                t = (z + (4 - s) + 8) % 8 if d == 0 else (z - (4 - s) + 8) % 8
                value = grid_f[j, t]
                if s > first:
                    z_copy(d, s - 1, j).wait_recv()
                    value = value + rx_z[d, s - 1, j].astype(F32)
                tx_z[d, s, j] = value.astype(BF16)
                z_copy(d, s, j).start()

    def x_copy(j):
        return pltpu.make_async_remote_copy(
            src_ref=tx_x.at[j], dst_ref=rx_x.at[j], send_sem=x_ss.at[j], recv_sem=x_rs.at[j],
            device_id=dev(dh=1), device_id_type=MESH)

    for j in range(4):
        z_copy(0, 3, j).wait_recv()
        z_copy(1, 3, j).wait_recv()
        value = grid_f[j, z] + rx_z[0, 3, j].astype(F32) + rx_z[1, 3, j].astype(F32)
        grid_f[j, z] = value
        tx_x[j] = value.astype(BF16)
        x_copy(j).start()

    for cp in fa_copies:
        cp.wait()

    def a_copy(j):
        yq = (y + (0, 1, 3, 2)[j]) % 4
        return pltpu.make_async_remote_copy(
            src_ref=resp.at[j], dst_ref=r_out.at[z, xl, y],
            send_sem=a_ss.at[j], recv_sem=a_rs.at[y],
            device_id=exchange_peer(yq), device_id_type=MESH)

    lane = lax.broadcasted_iota(jnp.int32, (1, 128), 1)
    second = (lane // 32) % 2 == 1
    sign = jnp.where(lane < 64, -1.0, 1.0).astype(F32)
    zh, zl = z // 4, z % 4
    s2, g0 = msq[zh], mdf[zh]
    fb_row = fbt[pl.ds(pair, 1), :]
    for j in range(4):
        slot = 2 * (0, 1, 3, 2)[j] + (core + xl) % 2
        x_copy(j).wait_recv()
        f = grid_f[j, z] + rx_x[j].astype(F32)
        fa0 = fas[slot, pl.ds(zl * 2, 1), :]
        fa1 = fas[slot, pl.ds(zl * 2 + 1, 1), :]
        w = jnp.where(second, fa1, fa0) + fb_row
        t = s2 - w * w
        g = g0 * w
        inv = 1.0 / (t * t + g * g)
        re = s2 * t * inv
        im = -s2 * g * inv
        out = (re * f + im * (sign * pltpu.roll(f, 64, 1))).astype(BF16)
        if j == 0:
            @pl.when(cross)
            def _():
                resp[j] = out
                a_copy(j).start()

            @pl.when(jnp.logical_not(cross))
            def _():
                r_out[z, xl, y] = out
        else:
            resp[j] = out
            a_copy(j).start()

    def a_arrival(yq):
        return pltpu.make_async_remote_copy(
            src_ref=resp.at[0], dst_ref=r_out.at[z, core, yq],
            send_sem=a_ss.at[0], recv_sem=a_rs.at[yq],
            device_id=dev(dc=1), device_id_type=MESH)

    for dy in range(1, 4):
        a_arrival((y + dy) % 4).wait_recv()

    @pl.when(cross)
    def _():
        a_arrival(y).wait_recv()

    def g_copy(d, dist, h):
        src = (z - dist + 8) % 8 if d == 0 else (z + dist) % 8
        part = r_out.at[src, core, pl.ds(2 * h, 2)]
        return pltpu.make_async_remote_copy(
            src_ref=part, dst_ref=part, send_sem=g_ss.at[d, dist, h], recv_sem=g_rs.at[d, dist, h],
            device_id=dev(dz=1 if d == 0 else -1), device_id_type=MESH)

    def g_arrival(d, dist, h):
        src = (z - dist - 1 + 8) % 8 if d == 0 else (z + dist + 1) % 8
        part = r_out.at[src, core, pl.ds(2 * h, 2)]
        return pltpu.make_async_remote_copy(
            src_ref=part, dst_ref=part, send_sem=g_ss.at[d, dist, h], recv_sem=g_rs.at[d, dist, h],
            device_id=dev(dc=1), device_id_type=MESH)

    def sib_chunk(n, dz, h, mine=True):
        part = r_out.at[(z + dz + 8) % 8, core if mine else 1 - core, pl.ds(2 * h, 2)]
        return pltpu.make_async_remote_copy(
            src_ref=part, dst_ref=part, send_sem=gs_ss.at[n], recv_sem=gs_rs.at[n],
            device_id=dev(dc=1), device_id_type=MESH)

    chunks = []
    for dist in range(4):
        for h in range(2):
            for d in range(2):
                if dist > 0:
                    g_arrival(d, dist - 1, h).wait_recv()
                if dist < 3 or d == h:
                    g_copy(d, dist, h).start()
                if dist > 0 or d == 0:
                    dz = -dist if d == 0 else dist
                    sib_chunk(len(chunks), dz, h).start()
                    chunks.append((dz, h))
    for h in range(2):
        g_arrival(h, 3, h).wait_recv()
        sib_chunk(len(chunks), -4, h).start()
        chunks.append((-4, h))

    for n, (dz, h) in enumerate(chunks):
        sib_chunk(n, dz, h, mine=False).wait_recv()

    def drain(j, _):
        sib_copy(j).wait_send()
        x_copy(j).wait_send()
        return 0

    lax.fori_loop(0, 4, drain, 0)
    for s in range(4):
        for j in range(4):
            for d in range(2):
                if s >= (0 if j % 2 == d else 1):
                    z_copy(d, s, j).wait_send()
    for j in range(1, 4):
        a_copy(j).wait_send()

    @pl.when(cross)
    def _():
        a_copy(0).wait_send()

    for dist in range(4):
        for h in range(2):
            for d in range(2):
                if dist < 3 or d == h:
                    g_copy(d, dist, h).wait_send()
    for n, (dz, h) in enumerate(chunks):
        sib_chunk(n, dz, h).wait_send()


def stress_kernel(st, r_in, out, rhs, acc):
    @pl.when(pl.program_id(0) == 0)
    def _():
        lane = lax.broadcasted_iota(jnp.int32, (1, 128), 1) // 32

        def arrange(n, _):
            zh, zl, hp = n // 8, (n // 2) % 4, n % 2
            blocks = [r_in[zh * 4 + zl, i % 2, hp * 2 + i // 2].astype(F32) for i in range(4)]
            for g in range(4):
                row = None
                for i in range(4):
                    part = blocks[i] if i == g else pltpu.roll(blocks[i], ((i - g) * 32) % 128, 1)
                    row = part if row is None else jnp.where(lane == i, part, row)
                idx = (g // 2) * 8 + zl * 2 + g % 2
                rhs[idx, zh, :, pl.ds(pl.multiple_of(hp * 128, 128), 128)] = row.astype(BF16)
            return 0

        lax.fori_loop(0, 16, arrange, 0)

    for ra in range(16):
        r = rhs[ra].reshape(2 * MH, 256)
        acc[:, ra, :] = lax.dot_general(
            st[...], r, (((1,), (0,)), ((), ())), preferred_element_type=F32)
    out[...] = acc[...].reshape(out.shape).astype(BF16)


def local(vel_a, vel_b, panel_modes, modal_stress, freq_a, freq_b, mode_freq, damping):
    va = jnp.transpose(vel_a, (2, 1, 0, 3)).reshape(48, KD)
    vb = jnp.transpose(vel_b, (2, 1, 0, 3)).reshape(192, KD)
    fa = jnp.broadcast_to(freq_a[:, None], (A8, 128))
    fbt = jnp.tile(freq_b.reshape(8, B32), (1, 4))
    mf = jnp.pad(mode_freq, (0, 2 * MH - M), constant_values=1.0)
    dm = jnp.pad(damping, (0, 2 * MH - M), constant_values=0.1)
    msq = jnp.broadcast_to((mf * mf)[:, None], (2 * MH, 128)).reshape(2, MH, 128)
    mdf = jnp.broadcast_to((2.0 * dm * mf)[:, None], (2 * MH, 128)).reshape(2, MH, 128)
    vm = pl.BlockSpec(memory_space=pltpu.VMEM)
    dma = pltpu.SemaphoreType.DMA
    r = pl.pallas_call(
        main_kernel,
        out_shape=jax.ShapeDtypeStruct((8, 2, 4, MH, 128), BF16),
        in_specs=[vm] * 7,
        out_specs=vm,
        scratch_shapes=[
            pltpu.VMEM((8, 48, KD), BF16),
            pltpu.VMEM((8, A8, 128), F32),
            pltpu.VMEM((KT, 9, B32, 128), F32),
            pltpu.VMEM((72, 128), F32),
            pltpu.VMEM((512, KD), BF16),
            pltpu.VMEM((4, 8, MH, 128), F32),
            pltpu.VMEM((4, 8, MH, 128), BF16),
            pltpu.VMEM((4, 8, MH, 128), BF16),
            pltpu.VMEM((2, 4, 4, MH, 128), BF16),
            pltpu.VMEM((2, 4, 4, MH, 128), BF16),
            pltpu.VMEM((4, MH, 128), BF16),
            pltpu.VMEM((4, MH, 128), BF16),
            pltpu.VMEM((4, MH, 128), BF16),
            dma((8,)), dma((8,)), dma((7,)), dma((7,)), dma((4,)), dma((4,)),
            dma((2, 4, 4)), dma((2, 4, 4)), dma((4,)), dma((4,)),
            dma((4,)), dma((4,)), dma((2, 4, 2)), dma((2, 4, 2)), dma((16,)), dma((16,)),
            dma((2,)),
        ],
        compiler_params=pltpu.CompilerParams(
            collective_id=0, has_side_effects=True, vmem_limit_bytes=48 * 1024 * 1024),
    )(va, vb, panel_modes, fa, fbt, msq, mdf)
    elements = modal_stress.shape[1]
    st = jnp.pad(modal_stress.T, ((0, 0), (0, 2 * MH - M)))
    tile = 128
    return pl.pallas_call(
        stress_kernel,
        out_shape=jax.ShapeDtypeStruct((elements, 2, A8, 256), BF16),
        grid=(elements // tile,),
        in_specs=[
            pl.BlockSpec((tile, 2 * MH), lambda i: (i, 0)),
            pl.BlockSpec((8, 2, 4, MH, 128), lambda i: (0, 0, 0, 0, 0)),
        ],
        out_specs=pl.BlockSpec((tile, 2, A8, 256), lambda i: (i, 0, 0, 0)),
        scratch_shapes=[
            pltpu.VMEM((16, 2, MH, 256), BF16),
            pltpu.VMEM((tile, 16, 256), F32),
        ],
        compiler_params=pltpu.CompilerParams(vmem_limit_bytes=48 * 1024 * 1024),
    )(st, r)


def solution(mesh):
    in_specs = (
        P("pair", None, None, "zone"),
        P("pair", None, None, "zone"),
        P(None, "zone"),
        P(None, "zone"),
        P("pair"),
        P(),
        P(),
        P(),
    )
    out_specs = P("zone", None, "pair", None)
    return jax.shard_map(local, mesh=mesh, in_specs=in_specs, out_specs=out_specs, check_vma=False)
```

time: 456 us -> 95.8 us (0.21)
  waiting for transfers between devices: 393 us -> 0 us
  Pallas kernels: 0 us -> 88.5 us
  other arithmetic: 21.4 us -> 0.71 us
  between operations: 13.5 us -> 0.06 us
  local copies, waits for them, and re-layouts: 16.4 us -> 6.22 us
  matrix products: 8.62 us -> 0 us
    psum x1 -> x0, waiting for transfers between devices: 273 us -> none  [local(): forces = lax.psum(flat_forces, 'zone')]
    all_gather x1 -> x0, waiting for transfers between devices: 120 us -> none  [local(): lax.all_gather(vel_b, 'pair', axis=0, tiled=True).astype(jnp.float32)]
    pallas_call x0 -> x2, Pallas kernels: none -> 88.5 us  [the longest x1 80.5 us: local(): pl.pallas_call(main_kernel, out_shape=jax.ShapeDtypeStruct((8, 2, 4, MH,...]
    another operation x2 -> x0, other arithmetic: 16.9 us -> none
    reshape x2 -> x0, local copies, waits for them, and re-layouts: 9.93 us -> none  [the longest x1 7.83 us: local(): return stress.reshape(element_count, 2, first_count, second_count)]
    dot_general x2 -> x0, matrix products: 8.62 us -> none  [the longest x1 5.26 us: local(): jnp.einsum('mk,rabk->mrab', panel_modes, pressure, preferred_element_type...]
  transfers between devices with their start and end apart: 2 -> 0, of which waited for: 2 -> 0; matrix products, arithmetic and copies ran while one was open for 0% -> 0% of each run, Pallas kernels for 0% -> 0%
where the time goes in v1:
time: 95.8 us; the launch traced here: 95.5 us
  Pallas kernels  88.5 us (92%)
  local copies, waits for them, and re-layouts  6.22 us (6%)
    pallas_call x1, Pallas kernels, local(): pl.pallas_call(main_kernel, out_shape=jax.ShapeDtypeStruct((8, 2, 4, MH,...  80.5 us
    pallas_call x1, Pallas kernels, local(): pl.pallas_call(stress_kernel, out_shape=jax.ShapeDtypeStruct((elements, 2...  8.01 us
    unnamed x3, local copies, waits for them, and re-layouts  2.17 us

profile of v1, /device:TPU:1, one launch (start us, length us, event | category | flops | bytes accessed | tf_op | source)
XLA Modules:
  0.0 95.5 jit_solution(14922875889413728546)
XLA Ops:
  0.0 0.7 multiply_multiply_fusion
  0.7 0.1 broadcast_in_dim.25
  0.8 0.1 broadcast_in_dim.11
  0.9 0.7 broadcast_in_dim.10.fa
  1.6 0.8 tile.10
  2.4 0.1 tile.12.fbt
  2.4 0.1 broadcast_in_dim.24.msq
  2.5 0.1 broadcast_in_dim.26.mdf
  2.6 0.9 copy.10
  3.6 1.1 %copy.9 = bf16[200,512]{0,1:T(8,128)(2,1)S(1)} copy(bf16[200,512]{1,0:T(8,128)(2,1)} %param.11) | data formatting | bytes 409600 | tf_op args[3]
  4.7 1.2 %copy.11 = bf16[3,2,32,1792]{3,2,1,0:T(8,128)(2,1)S(1)} copy(bf16[3,2,32,1792]{3,1,0,2:T(2,128)(2,1)} %bitcast.8) | data formatting | bytes 1376256 | tf_op jit(solution)/shard_map/transpose | solution.py:401
  5.9 0.0 copy-start
  5.9 1.1 %copy-done = bf16[200,1792]{1,0:T(8,128)(2,1)S(1)} copy-done((bf16[200,1792]{1,0:T(8,128)(2,1)S(1)}, bf16[200,1792]{1,0:T(8,128)(2,1)}, u32[]{:S(2)}) %copy-start) | copy-done | bytes 716824
  7.0 80.5 %shard_map.82.r_in = bf16[8,2,4,104,128]{4,3,2,1,0:T(8,128)(2,1)S(1)} custom-call(bf16[48,1792]{1,0:T(8,128)(2,1)S(1)} %bitcast.6, bf16[192,1792]{1,0:T(8,128)(2,1)S(1)} %bitcast.5, bf16[200,1792]{1,0:T(8,128)(2,1)S(1)} %copy-done, f32[8,128]{1,0:T(8,128)S(1)} %broadcast_in_dim.10.fa, f32[8,128]{1,0:T(8,128)S(1)} %tile.12.fbt, ...), custom_call_target="tpu_custom_call" | custom-call | tf_op jit(solution)/shard_map/pallas_call | solution.py:410
  87.5 8.0 %shard_map.83 = bf16[512,2,8,256]{3,2,1,0:T(8,128)(2,1)} custom-call(bf16[512,208]{1,0:T(8,128)(2,1)S(1)} %pad.11.st, bf16[8,2,4,104,128]{4,3,2,1,0:T(8,128)(2,1)S(1)} %shard_map.82.r_in), custom_call_target="tpu_custom_call" | custom-call | tf_op jit(solution)/shard_map/pallas_call | solution.py:440
  (2 shorter events, 0.0 us)
Async XLA Ops:
  5.9 1.1 %copy-start = (bf16[200,1792]{1,0:T(8,128)(2,1)S(1)}, bf16[200,1792]{1,0:T(8,128)(2,1)}, u32[]{:S(2)}) copy-start(bf16[200,1792]{1,0:T(8,128)(2,1)} %modes.1) | copy-start | bytes 2150404

commit v2 on v0

v2 whole, which is shorter than its diff:
```python
import functools

import jax
import jax.numpy as jnp
from jax import lax
from jax.experimental import pallas as pl
from jax.experimental.pallas import tpu as pltpu
from jax.sharding import PartitionSpec as P

MESH = pl.DeviceIdType.MESH
F32 = jnp.float32
BF16 = jnp.bfloat16

A8 = 8
B32 = 32
KD = 1792
KT = KD // 128
M = 200
FM, FD = 264, 464
MH = 104
EVEN = ((0, 0), (0, 1), (2, 0), (2, 1))
ODD = ((1, 0), (3, 0), (1, 1), (3, 1))


def main_kernel(
    va, vb, modes_in, small_in,
    rhs,
    small, modes, r_in, vel, fas, msq, mdf, vf, uf, prs0, prs1, grid_f,
    tx_sib, rx_sib, tx_z, rx_z, tx_x, rx_x, resp,
    vel_ss, vel_rs, fa_ss, fa_rs, sib_ss, sib_rs, z_ss, z_rs, x_ss, x_rs,
    a_ss, a_rs, g_ss, g_rs, gs_ss, gs_rs, loc_sem,
):
    pair = lax.axis_index("pair")
    zone = lax.axis_index("zone")
    y, xl = pair // 2, pair % 2
    core, z, xh = zone % 2, (zone // 2) % 8, zone // 16

    def dev(dy=0, dx=0, dz=0, dh=0, dc=0):
        return (
            ((y + dy) % 4) * 2 + (xl + dx) % 2,
            (((xh + dh) % 2) * 8 + (z + dz + 8) % 8) * 2 + (core + dc) % 2,
        )

    cross = (y + core) % 2

    def group(j):
        dy = (1 - cross) * EVEN[j][0] + cross * ODD[j][0]
        dx = (1 - cross) * EVEN[j][1] + cross * ODD[j][1]
        return dy, dx

    def exchange_peer(j):
        dy, dx = group(j)
        return (((y + dy) % 4) * 2 + (xl + dx) % 2, (xh * 8 + z) * 2 + y % 2)

    crossed = cross == 1

    barrier = pltpu.get_barrier_semaphore()
    pair_peers = [(dy, dx) for dy in range(4) for dx in range(2) if (dy, dx) != (0, 0)]
    for dy, dx in pair_peers:
        pl.semaphore_signal(barrier, inc=1, device_id=dev(dy=dy, dx=dx), device_id_type=MESH)
    for kw in (dict(dc=1), dict(dz=1), dict(dz=-1), dict(dz=2), dict(dz=-2), dict(dh=1)):
        pl.semaphore_signal(barrier, inc=1, device_id=dev(**kw), device_id_type=MESH)

    @pl.when(crossed)
    def _():
        for j in range(4):
            pl.semaphore_signal(barrier, inc=1, device_id=exchange_peer(j), device_id_type=MESH)

    own_vel = pltpu.make_async_copy(va, vel.at[0], loc_sem.at[0])
    own_vel.start()
    own_modes = pltpu.make_async_copy(modes_in, modes, loc_sem.at[1])
    own_modes.start()
    own_small = pltpu.make_async_copy(small_in, small, loc_sem.at[2])
    own_small.start()
    pl.semaphore_wait(barrier, 13 + 4 * cross)

    def vel_copy(src, dst, k, to, half=None):
        s = va if src == 0 else vel.at[src] if half is None else vel.at[src, :, pl.ds(half, KD // 2)]
        d = vel.at[dst] if half is None else vel.at[dst, :, pl.ds(half, KD // 2)]
        return pltpu.make_async_remote_copy(
            src_ref=s, dst_ref=d, send_sem=vel_ss.at[k], recv_sem=vel_rs.at[k],
            device_id=to, device_id_type=MESH)

    c_x = vel_copy(0, 1, 0, dev(dx=1))
    c_yp = vel_copy(0, 6, 1, dev(dy=1))
    c_ym = vel_copy(0, 2, 2, dev(dy=3))
    c_xyp = vel_copy(1, 7, 3, dev(dy=1))
    c_xym = vel_copy(1, 3, 4, dev(dy=3))
    c_fyp = vel_copy(6, 4, 5, dev(dy=1), 0)
    c_fym = vel_copy(2, 4, 6, dev(dy=3), KD // 2)
    c_x2 = vel_copy(4, 5, 7, dev(dx=1), 0)
    c_x3 = vel_copy(4, 5, 8, dev(dx=1), KD // 2)
    c_yp.start()
    c_ym.start()
    c_x.start()
    own_small.wait()
    for a in range(A8):
        fas[0, a:a + 1, :] = jnp.full((1, 128), small[a], F32)
    fa_copies = []
    for n, (dy, dx) in enumerate(pair_peers):
        slot = 2 * ((4 - dy) % 4) + dx
        cp = pltpu.make_async_remote_copy(
            src_ref=fas.at[0], dst_ref=fas.at[slot], send_sem=fa_ss.at[n], recv_sem=fa_rs.at[n],
            device_id=dev(dy=dy, dx=dx), device_id_type=MESH)
        cp.start()
        fa_copies.append(cp)

    def zero_pad(n, _):
        grid_f[n // 4, 4 + n % 4, 96:104, :] = jnp.zeros((8, 128), F32)
        return 0

    lax.fori_loop(0, 20, zero_pad, 0)

    def mode_row(n, _):
        for h in range(2):
            f = small[FM + h * MH + n]
            msq[h, pl.ds(n, 1), :] = jnp.full((1, 128), f * f, F32)
            mdf[h, pl.ds(n, 1), :] = jnp.full((1, 128), 2.0 * small[FD + h * MH + n] * f, F32)
        return 0

    lax.fori_loop(0, 96, mode_row, 0)
    for n in range(96, 104):
        f = small[FM + n]
        msq[0, n:n + 1, :] = jnp.full((1, 128), f * f, F32)
        mdf[0, n:n + 1, :] = jnp.full((1, 128), 2.0 * small[FD + n] * f, F32)
    msq[1, 96:104, :] = jnp.ones((8, 128), F32)
    mdf[1, 96:104, :] = jnp.ones((8, 128), F32)

    def prep(kt, _):
        lanes = pl.ds(pl.multiple_of(kt * 128, 128), 128)
        for c in range(3):
            vr = vb[c * 64:c * 64 + 32, lanes].astype(F32)
            vi = vb[c * 64 + 32:c * 64 + 64, lanes].astype(F32)
            vf[kt, c * 3] = vr
            vf[kt, c * 3 + 1] = vi - vr
            vf[kt, c * 3 + 2] = vr + vi
        return 0

    lax.fori_loop(0, KT, prep, 0)

    def sib_copy(j):
        return pltpu.make_async_remote_copy(
            src_ref=tx_sib.at[j], dst_ref=rx_sib.at[j], send_sem=sib_ss.at[j], recv_sem=sib_rs.at[j],
            device_id=dev(dc=1), device_id_type=MESH)

    def mine(dx):
        return cross == dx

    def send_sibling(j, dx):
        @pl.when(jnp.logical_not(mine(dx)))
        def _():
            def one(t, _):
                tx_sib[j, t] = grid_f[4, t].astype(BF16)
                return 0

            lax.fori_loop(0, 8, one, 0)
            sib_copy(j).start()

    def z_copy(d, n, j):
        hop = (1, 2, 1, 2)[n]
        return pltpu.make_async_remote_copy(
            src_ref=tx_z.at[d, n, j], dst_ref=rx_z.at[d, n, j],
            send_sem=z_ss.at[d, n, j], recv_sem=z_rs.at[d, n, j],
            device_id=dev(dz=hop if d == 0 else -hop), device_id_type=MESH)

    def x_copy(j):
        return pltpu.make_async_remote_copy(
            src_ref=tx_x.at[j], dst_ref=rx_x.at[j], send_sem=x_ss.at[j], recv_sem=x_rs.at[j],
            device_id=dev(dh=1), device_id_type=MESH)

    def a_copy(j):
        return pltpu.make_async_remote_copy(
            src_ref=resp.at[j], dst_ref=r_in.at[z, y % 2, (y // 2) * 2 + xl],
            send_sem=a_ss.at[j], recv_sem=a_rs.at[j],
            device_id=exchange_peer(j), device_id_type=MESH)

    def origin(j):
        dy, dx = group(j)
        return ((y + 4 - dy) % 4 // 2) * 2 + (xl + dx) % 2

    def a_arrival(j):
        return pltpu.make_async_remote_copy(
            src_ref=resp.at[0], dst_ref=r_in.at[z, core, origin(j)],
            send_sem=a_ss.at[j], recv_sem=a_rs.at[j],
            device_id=dev(dc=1), device_id_type=MESH)

    def g_copy(d, far, j):
        back = 0 if far <= 2 else 2
        src = (z - back + 8) % 8 if d == 0 else (z + back) % 8
        hop = far - back
        part = r_in.at[src, core, origin(j)]
        return pltpu.make_async_remote_copy(
            src_ref=part, dst_ref=part, send_sem=g_ss.at[d, far - 1, j], recv_sem=g_rs.at[d, far - 1, j],
            device_id=dev(dz=hop if d == 0 else -hop), device_id_type=MESH)

    def g_arrival(d, far, j):
        src = (z - far + 8) % 8 if d == 0 else (z + far) % 8
        part = r_in.at[src, core, origin(j)]
        return pltpu.make_async_remote_copy(
            src_ref=part, dst_ref=part, send_sem=g_ss.at[d, far - 1, j], recv_sem=g_rs.at[d, far - 1, j],
            device_id=dev(dc=1), device_id_type=MESH)

    def sib_chunk(dz, j, own=True):
        if own:
            where = origin(j)
        else:
            other = 1 - cross
            dy = (1 - other) * EVEN[j][0] + other * ODD[j][0]
            dx = (1 - other) * EVEN[j][1] + other * ODD[j][1]
            where = ((y + 4 - dy) % 4 // 2) * 2 + (xl + dx) % 2
        part = r_in.at[(z + dz + 8) % 8, core if own else 1 - core, where]
        return pltpu.make_async_remote_copy(
            src_ref=part, dst_ref=part, send_sem=gs_ss.at[dz + 4, j], recv_sem=gs_rs.at[dz + 4, j],
            device_id=dev(dc=1), device_id_type=MESH)

    lane = lax.broadcasted_iota(jnp.int32, (1, 128), 1)
    second = (lane // 32) % 2 == 1
    sign = jnp.where(lane < 64, -1.0, 1.0).astype(F32)

    def part_for(j, t):
        return grid_f[j, t] + rx_sib[j, t].astype(F32)

    def far_side(d, j):
        return j % 2 == d

    def z_first(j):
        sib_copy(j).wait_recv()
        for n, dist in ((0, 3), (1, 4), (2, 1)):
            for d in range(2):
                if n == 1 and not far_side(d, j):
                    continue
                t = (z + dist) % 8 if d == 0 else (z - dist + 8) % 8
                tx_z[d, n, j] = part_for(j, t).astype(BF16)
                z_copy(d, n, j).start()

    def z_second(j):
        for d in range(2):
            t = (z + 2) % 8 if d == 0 else (z - 2 + 8) % 8
            value = part_for(j, t)
            for n in range(2):
                if n == 0 or far_side(d, j):
                    z_copy(d, n, j).wait_recv()
                    value = value + rx_z[d, n, j].astype(F32)
            tx_z[d, 3, j] = value.astype(BF16)
            z_copy(d, 3, j).start()

    def x_step(j):
        value = part_for(j, z)
        for n in (2, 3):
            for d in range(2):
                z_copy(d, n, j).wait_recv()
                value = value + rx_z[d, n, j].astype(F32)
        grid_f[j, z] = value
        tx_x[j] = value.astype(BF16)
        x_copy(j).start()

    def respond(j):
        if j == 0:
            for cp in fa_copies:
                cp.wait()
        zh, zl = z // 4, z % 4
        gy, gx = group(j)
        slot = 2 * gy + gx
        s2 = msq[zh]
        x_copy(j).wait_recv()
        f = grid_f[j, z] + rx_x[j].astype(F32)
        fb_row = jnp.zeros((1, 128), F32)
        for b in range(B32):
            fb_row = jnp.where(lane % B32 == b, small[A8 + pair * B32 + b], fb_row)
        w = jnp.where(second, fas[slot, pl.ds(zl * 2 + 1, 1), :], fas[slot, pl.ds(zl * 2, 1), :]) + fb_row
        t = s2 - w * w
        g = mdf[zh] * w
        inv = 1.0 / (t * t + g * g)
        re = s2 * t * inv
        im = -s2 * g * inv
        out = (re * f + im * (sign * pltpu.roll(f, 64, 1))).astype(BF16)
        if j == 0:
            @pl.when(crossed)
            def _():
                resp[j] = out
                a_copy(j).start()

            @pl.when(jnp.logical_not(crossed))
            def _():
                r_in[z, y % 2, (y // 2) * 2 + xl] = out
        else:
            resp[j] = out
            a_copy(j).start()

    def g_first(j):
        if j == 0:
            @pl.when(crossed)
            def _():
                a_arrival(0).wait_recv()
        else:
            a_arrival(j).wait_recv()
        for far in (2, 1):
            for d in range(2):
                g_copy(d, far, j).start()
        sib_chunk(0, j).start()

    def g_second(j):
        for d in range(2):
            g_arrival(d, 2, j).wait_recv()
            g_copy(d, 3, j).start()
            if far_side(d, j):
                g_copy(d, 4, j).start()
        for d in range(2):
            sib_chunk(2 if d else -2, j).start()
        for d in range(2):
            g_arrival(d, 1, j).wait_recv()
            sib_chunk(1 if d else -1, j).start()

    def g_last(j):
        for d in range(2):
            g_arrival(d, 3, j).wait_recv()
            sib_chunk(3 if d else -3, j).start()
        g_arrival(j % 2, 4, j).wait_recv()
        sib_chunk(-4, j).start()

    def arrange(dz):
        for j in range(4):
            sib_chunk(dz, j, own=False).wait_recv()
        zc = (z + dz + 8) % 8
        zh, zl = zc // 4, zc % 4
        low, even = lane < 64, (lane // 32) % 2 == 0

        def half(hp, _):
            b = [r_in[zc, i // 2, hp * 2 + i % 2].astype(F32) for i in range(4)]
            u = [None] * 4
            for i in range(2):
                u[i] = jnp.where(low, b[i], pltpu.roll(b[i + 2], 64, 1))
                u[i + 2] = jnp.where(low, pltpu.roll(b[i], 64, 1), b[i + 2])
            w = [None] * 4
            for i in (0, 2):
                w[i] = jnp.where(even, u[i], pltpu.roll(u[i + 1], 32, 1))
                w[i + 1] = jnp.where(even, pltpu.roll(u[i], 96, 1), u[i + 1])
            for g in range(4):
                idx = (g // 2) * 8 + zl * 2 + g % 2
                rhs[idx, zh, :, pl.ds(pl.multiple_of(hp * 128, 128), 128)] = w[g].astype(BF16)
            return 0

        lax.fori_loop(0, 2, half, 0)

    STAGES = (z_first, z_second, x_step, respond, g_first, g_second, g_last)

    def stage(j, k):
        STAGES[k](j)
        if j == 3 and k == 5:
            arrange(0)
        if j == 3 and k == 6:
            for dz in (1, -1, 2, -2):
                arrange(dz)

    WHEN = ((4, 6, 8, 9, 10, 11, 12), (6, 8, 9, 10, 11, 12, 13),
            (8, 9, 10, 11, 12, 13, 14), (10, 11, 12, 13, 14, 15, 16))

    def events(t):
        return [(j, WHEN[j].index(t)) for j in (3, 2, 1, 0) if t in WHEN[j]]

    def forces(prs, h, dst):
        f = lax.dot_general(
            modes[...], prs[pl.ds(pl.multiple_of(h * 256, 256), 256), :], (((1,), (1,)), ((), ())),
            preferred_element_type=F32)
        for n in range(2):
            grid_f[dst, 2 * h + n] = f[0:104, n * 128:n * 128 + 128]
            grid_f[dst, 4 + 2 * h + n, 0:96] = f[104:200, n * 128:n * 128 + 128]

    def pressure(prs, slot, kt, k):
        lanes = pl.ds(pl.multiple_of(kt * 128, 128), 128)
        for c in range(3):
            both = vel[slot, c * 16:c * 16 + 16, lanes].astype(F32)
            ur, ui = both[0:8] * -0.5, both[8:16] * -0.5
            uf[k, c * 24:c * 24 + 8] = ur
            uf[k, c * 24 + 8:c * 24 + 16] = ui
            uf[k, c * 24 + 16:c * 24 + 24] = ur + ui
        for half in range(2):
            v = [vf[kt, n, half * 16:half * 16 + 16, :] for n in range(9)]
            for a in range(A8):
                row = (a // 2) * 128 + (a % 2) * 32 + half * 16
                k1 = k2 = k3 = None
                for c in range(3):
                    ur = uf[k, c * 24 + a:c * 24 + a + 1, :]
                    ui = uf[k, c * 24 + 8 + a:c * 24 + 8 + a + 1, :]
                    us = uf[k, c * 24 + 16 + a:c * 24 + 16 + a + 1, :]
                    t1, t2, t3 = v[c * 3] * us, v[c * 3 + 1] * ur, v[c * 3 + 2] * ui
                    k1 = t1 if k1 is None else k1 + t1
                    k2 = t2 if k2 is None else k2 + t2
                    k3 = t3 if k3 is None else k3 + t3
                prs[row:row + 16, lanes] = (k1 - k3).astype(BF16)
                prs[row + 64:row + 80, lanes] = (k1 + k2).astype(BF16)

    own_modes.wait()
    own_vel.wait()
    bufs = (prs0, prs1)

    def double_block(j, _):
        slots = (j % 2 + 4 * (j // 2), 2 + 4 * (j % 2) + j // 2)
        for dx in range(2):
            slot = slots[dx]
            if dx == 0:
                @pl.when(j == 3)
                def _():
                    c_x2.wait_recv()
                    c_x3.wait_recv()
            else:
                @pl.when(j == 0)
                def _():
                    c_yp.wait_recv()
                    c_fyp.start()
                    c_ym.wait_recv()
                    c_fym.start()
                    c_x.wait_recv()
                    c_xym.start()
                    c_xyp.start()

                @pl.when(j == 1)
                def _():
                    c_fyp.wait_recv()
                    c_x2.start()
                    c_fym.wait_recv()
                    c_x3.start()

                @pl.when(j == 2)
                def _():
                    c_xym.wait_recv()

                @pl.when(j == 3)
                def _():
                    c_xyp.wait_recv()

            @pl.when(j >= 1)
            def _():
                send_sibling(j - 1, dx)

            for jj in range(4):
                for t in events(2 * jj + dx):
                    @pl.when(j == jj)
                    def _():
                        stage(*t)

            if dx == 0:
                dst = jnp.where(jnp.logical_and(mine(1), j >= 1), jnp.maximum(j - 1, 0), 4)
            else:
                dst = jnp.where(mine(0), j, 4)

            def half(h, _):
                forces(bufs[1 - dx], h, dst)
                for k in range(7):
                    pressure(bufs[dx], slot, h * 7 + k, k)
                return 0

            lax.fori_loop(0, 2, half, 0)
        return 0

    lax.fori_loop(0, 4, double_block, 0)

    send_sibling(3, 0)
    last = jnp.where(mine(1), 3, 4)

    def last_half(h, _):
        forces(prs1, h, last)
        return 0

    lax.fori_loop(0, 2, last_half, 0)
    send_sibling(3, 1)
    for t in range(8, 17):
        for j, k in events(t):
            stage(j, k)
    for dz in (3, -3, -4):
        arrange(dz)

    for cp in (c_x, c_yp, c_ym, c_xyp, c_xym, c_fyp, c_fym, c_x2, c_x3):
        cp.wait_send()

    def drain(j, _):
        sib_copy(j).wait_send()
        x_copy(j).wait_send()
        return 0

    lax.fori_loop(0, 4, drain, 0)
    for j in range(4):
        for n in range(4):
            for d in range(2):
                if n != 1 or far_side(d, j):
                    z_copy(d, n, j).wait_send()
    for j in range(1, 4):
        a_copy(j).wait_send()

    @pl.when(crossed)
    def _():
        a_copy(0).wait_send()

    for j in range(4):
        for far in range(1, 5):
            for d in range(2):
                if far < 4 or far_side(d, j):
                    g_copy(d, far, j).wait_send()
        for dz in range(-4, 4):
            sib_chunk(dz, j).wait_send()


def stress_kernel(ms, rhs, out, acc):
    for ra in range(16):
        r = rhs[ra].reshape(2 * MH, 256)[:M]
        acc[:, ra, :] = lax.dot_general(
            ms[...], r, (((0,), (0,)), ((), ())), preferred_element_type=F32)
    out[...] = acc[...].reshape(out.shape).astype(BF16)


def local(vel_a, vel_b, panel_modes, modal_stress, freq_a, freq_b, mode_freq, damping):
    va = jnp.transpose(vel_a, (2, 1, 0, 3)).reshape(48, KD)
    vb = jnp.transpose(vel_b, (2, 1, 0, 3)).reshape(192, KD)
    small = jnp.concatenate([freq_a, freq_b, mode_freq, damping])
    vm = pl.BlockSpec(memory_space=pltpu.VMEM)
    hbm = pl.BlockSpec(memory_space=pltpu.HBM)
    dma = pltpu.SemaphoreType.DMA
    r = pl.pallas_call(
        main_kernel,
        out_shape=jax.ShapeDtypeStruct((16, 2, MH, 256), BF16),
        in_specs=[vm, vm, hbm, hbm],
        out_specs=vm,
        scratch_shapes=[
            pltpu.SMEM((A8 + 256 + 2 * M,), F32),
            pltpu.VMEM((M, KD), BF16),
            pltpu.VMEM((8, 2, 4, MH, 128), BF16),
            pltpu.VMEM((8, 48, KD), BF16),
            pltpu.VMEM((8, A8, 128), F32),
            pltpu.VMEM((2, MH, 128), F32),
            pltpu.VMEM((2, MH, 128), F32),
            pltpu.VMEM((KT, 9, B32, 128), F32),
            pltpu.VMEM((7, 72, 128), F32),
            pltpu.VMEM((512, KD), BF16),
            pltpu.VMEM((512, KD), BF16),
            pltpu.VMEM((5, 8, MH, 128), F32),
            pltpu.VMEM((4, 8, MH, 128), BF16),
            pltpu.VMEM((4, 8, MH, 128), BF16),
            pltpu.VMEM((2, 4, 4, MH, 128), BF16),
            pltpu.VMEM((2, 4, 4, MH, 128), BF16),
            pltpu.VMEM((4, MH, 128), BF16),
            pltpu.VMEM((4, MH, 128), BF16),
            pltpu.VMEM((4, MH, 128), BF16),
            dma((9,)), dma((9,)), dma((7,)), dma((7,)), dma((4,)), dma((4,)),
            dma((2, 4, 4)), dma((2, 4, 4)), dma((4,)), dma((4,)),
            dma((4,)), dma((4,)), dma((2, 4, 4)), dma((2, 4, 4)), dma((8, 4)), dma((8, 4)),
            dma((3,)),
        ],
        compiler_params=pltpu.CompilerParams(
            collective_id=0, has_side_effects=True, vmem_limit_bytes=48 * 1024 * 1024),
    )(va, vb, panel_modes, small)
    elements = modal_stress.shape[1]
    tile = 128
    return pl.pallas_call(
        stress_kernel,
        out_shape=jax.ShapeDtypeStruct((elements, 2, A8, 256), BF16),
        grid=(elements // tile,),
        in_specs=[
            pl.BlockSpec((M, tile), lambda i: (0, i)),
            pl.BlockSpec((16, 2, MH, 256), lambda i: (0, 0, 0, 0)),
        ],
        out_specs=pl.BlockSpec((tile, 2, A8, 256), lambda i: (i, 0, 0, 0)),
        scratch_shapes=[pltpu.VMEM((tile, 16, 256), F32)],
        compiler_params=pltpu.CompilerParams(vmem_limit_bytes=48 * 1024 * 1024),
    )(modal_stress, r)


def solution(mesh):
    in_specs = (
        P("pair", None, None, "zone"),
        P("pair", None, None, "zone"),
        P(None, "zone"),
        P(None, "zone"),
        P("pair"),
        P(),
        P(),
        P(),
    )
    out_specs = P("zone", None, "pair", None)
    return jax.shard_map(local, mesh=mesh, in_specs=in_specs, out_specs=out_specs, check_vma=False)
```

time: 456 us -> 76 us (0.17)
  waiting for transfers between devices: 393 us -> 0 us
  Pallas kernels: 0 us -> 71.8 us
  other arithmetic: 21.4 us -> 0.83 us
  between operations: 13.5 us -> 0.04 us
  local copies, waits for them, and re-layouts: 16.4 us -> 3.22 us
  matrix products: 8.62 us -> 0 us
    psum x1 -> x0, waiting for transfers between devices: 273 us -> none  [local(): forces = lax.psum(flat_forces, 'zone')]
    all_gather x1 -> x0, waiting for transfers between devices: 120 us -> none  [local(): lax.all_gather(vel_b, 'pair', axis=0, tiled=True).astype(jnp.float32)]
    pallas_call x0 -> x2, Pallas kernels: none -> 71.8 us  [the longest x1 66 us: local(): pl.pallas_call(main_kernel, out_shape=jax.ShapeDtypeStruct((16, 2, MH, 25...]
    another operation x2 -> x0, other arithmetic: 16.9 us -> none
    reshape x2 -> x0, local copies, waits for them, and re-layouts: 9.93 us -> none  [the longest x1 7.83 us: local(): return stress.reshape(element_count, 2, first_count, second_count)]
    dot_general x2 -> x0, matrix products: 8.62 us -> none  [the longest x1 5.26 us: local(): jnp.einsum('mk,rabk->mrab', panel_modes, pressure, preferred_element_type...]
  transfers between devices with their start and end apart: 2 -> 0, of which waited for: 2 -> 0; matrix products, arithmetic and copies ran while one was open for 0% -> 0% of each run, Pallas kernels for 0% -> 0%
where the time goes in v2:
time: 76 us; the launch traced here: 75.8 us
  Pallas kernels  71.8 us (94%)
  local copies, waits for them, and re-layouts  3.22 us (4%)
  other arithmetic  0.83 us (1%)
    pallas_call x1, Pallas kernels, local(): pl.pallas_call(main_kernel, out_shape=jax.ShapeDtypeStruct((16, 2, MH, 25...  66 us
    pallas_call x1, Pallas kernels, local(): pl.pallas_call(stress_kernel, out_shape=jax.ShapeDtypeStruct((elements, 2...  5.8 us

profile of v2, /device:TPU:1, one launch (start us, length us, event | category | flops | bytes accessed | tf_op | source)
XLA Modules:
  0.0 75.8 jit_solution(14834503048202490994)
XLA Ops:
  0.0 0.0 copy-start.1
  0.0 0.8 %pad_maximum_fusion.small_in = f32[664]{0:T(1024)S(1)} fusion(f32[200]{0:T(256)} %param.15, f32[200]{0:T(256)} %param.14, f32[256]{0:T(256)} %param.13, f32[8]{0:T(128)} %param.12), kind=kLoop, calls=%fused_computation | loop fusion | flops 1992 | bytes 5312 | tf_op jit(solution)/shard_map/concatenate | solution.py:514
  0.8 0.9 %copy.9 = bf16[3,2,8,1792]{3,2,1,0:T(8,128)(2,1)S(1)} copy(bf16[3,2,8,1792]{3,1,0,2:T(2,128)(2,1)} %bitcast.7) | data formatting | bytes 344064 | tf_op jit(solution)/shard_map/transpose | solution.py:512
  1.8 1.2 %copy.10 = bf16[3,2,32,1792]{3,2,1,0:T(8,128)(2,1)S(1)} copy(bf16[3,2,32,1792]{3,1,0,2:T(2,128)(2,1)} %bitcast.6) | data formatting | bytes 1376256 | tf_op jit(solution)/shard_map/transpose | solution.py:513
  3.0 0.0 copy-start
  3.0 1.1 %copy-done = bf16[200,1792]{1,0:T(8,128)(2,1)S(1)} copy-done((bf16[200,1792]{1,0:T(8,128)(2,1)S(1)}, bf16[200,1792]{1,0:T(8,128)(2,1)}, u32[]{:S(2)}) %copy-start) | copy-done | bytes 716824
  4.1 66.0 %shard_map.82.rhs = bf16[16,2,104,256]{3,2,1,0:T(8,128)(2,1)S(1)} custom-call(bf16[48,1792]{1,0:T(8,128)(2,1)S(1)} %bitcast.5, bf16[192,1792]{1,0:T(8,128)(2,1)S(1)} %bitcast.4, bf16[200,1792]{1,0:T(8,128)(2,1)S(1)} %copy-done, f32[664]{0:T(1024)S(1)} %pad_maximum_fusion.small_in), custom_call_target="tpu_custom_call" | custom-call | tf_op jit(solution)/shard_map/pallas_call | solution.py:518
  70.0 0.0 copy-done.1
  70.0 5.8 %shard_map.83 = bf16[512,2,8,256]{3,2,1,0:T(8,128)(2,1)} custom-call(bf16[200,512]{1,0:T(8,128)(2,1)S(1)} %copy-done.1, bf16[16,2,104,256]{3,2,1,0:T(8,128)(2,1)S(1)} %shard_map.82.rhs), custom_call_target="tpu_custom_call" | custom-call | tf_op jit(solution)/shard_map/pallas_call | solution.py:553
Async XLA Ops:
  0.0 70.0 %copy-start.1 = (bf16[200,512]{1,0:T(8,128)(2,1)S(1)}, bf16[200,512]{1,0:T(8,128)(2,1)}, u32[]{:S(2)}) copy-start(bf16[200,512]{1,0:T(8,128)(2,1)} %ms.1) | copy-start | bytes 614404
  3.0 1.1 %copy-start = (bf16[200,1792]{1,0:T(8,128)(2,1)S(1)}, bf16[200,1792]{1,0:T(8,128)(2,1)}, u32[]{:S(2)}) copy-start(bf16[200,1792]{1,0:T(8,128)(2,1)} %modes_in.1) | copy-start | bytes 2150404

commit v3 on v2

--- a/solution.py
+++ b/solution.py
@@ -25,9 +25,9 @@
 def main_kernel(
     va, vb, modes_in, small_in,
     rhs,
-    small, modes, r_in, vel, fas, msq, mdf, vf, uf, prs0, prs1, grid_f,
-    tx_sib, rx_sib, tx_z, rx_z, tx_x, rx_x, resp,
-    vel_ss, vel_rs, fa_ss, fa_rs, sib_ss, sib_rs, z_ss, z_rs, x_ss, x_rs,
+    small, modes, r_in, vel, msq, mdf, vf, uf, prs0, prs1, grid_f,
+    tx_sib, rx_sib, tx_z, rx_z, tx_a, rx_a,
+    vel_ss, vel_rs, sib_ss, sib_rs, z_ss, z_rs,
     a_ss, a_rs, g_ss, g_rs, gs_ss, gs_rs, loc_sem,
 ):
     pair = lax.axis_index("pair")
@@ -48,9 +48,9 @@
         dx = (1 - cross) * EVEN[j][1] + cross * ODD[j][1]
         return dy, dx
 
-    def exchange_peer(j):
+    def exchange_peer(j, dh=0):
         dy, dx = group(j)
-        return (((y + dy) % 4) * 2 + (xl + dx) % 2, (xh * 8 + z) * 2 + y % 2)
+        return (((y + dy) % 4) * 2 + (xl + dx) % 2, (((xh + dh) % 2) * 8 + z) * 2 + y % 2)
 
     crossed = cross == 1
 
@@ -58,8 +58,11 @@
     pair_peers = [(dy, dx) for dy in range(4) for dx in range(2) if (dy, dx) != (0, 0)]
     for dy, dx in pair_peers:
         pl.semaphore_signal(barrier, inc=1, device_id=dev(dy=dy, dx=dx), device_id_type=MESH)
-    for kw in (dict(dc=1), dict(dz=1), dict(dz=-1), dict(dz=2), dict(dz=-2), dict(dh=1)):
+    for kw in (dict(dc=1), dict(dz=1), dict(dz=-1), dict(dz=2), dict(dz=-2)):
         pl.semaphore_signal(barrier, inc=1, device_id=dev(**kw), device_id_type=MESH)
+
+    for j in range(4):
+        pl.semaphore_signal(barrier, inc=1, device_id=exchange_peer(j, 1), device_id_type=MESH)
 
     @pl.when(crossed)
     def _():
@@ -72,7 +75,7 @@
     own_modes.start()
     own_small = pltpu.make_async_copy(small_in, small, loc_sem.at[2])
     own_small.start()
-    pl.semaphore_wait(barrier, 13 + 4 * cross)
+    pl.semaphore_wait(barrier, 16 + 4 * cross)
 
     def vel_copy(src, dst, k, to, half=None):
         s = va if src == 0 else vel.at[src] if half is None else vel.at[src, :, pl.ds(half, KD // 2)]
@@ -94,17 +97,6 @@
     c_ym.start()
     c_x.start()
     own_small.wait()
-    for a in range(A8):
-        fas[0, a:a + 1, :] = jnp.full((1, 128), small[a], F32)
-    fa_copies = []
-    for n, (dy, dx) in enumerate(pair_peers):
-        slot = 2 * ((4 - dy) % 4) + dx
-        cp = pltpu.make_async_remote_copy(
-            src_ref=fas.at[0], dst_ref=fas.at[slot], send_sem=fa_ss.at[n], recv_sem=fa_rs.at[n],
-            device_id=dev(dy=dy, dx=dx), device_id_type=MESH)
-        cp.start()
-        fa_copies.append(cp)
-
     def zero_pad(n, _):
         grid_f[n // 4, 4 + n % 4, 96:104, :] = jnp.zeros((8, 128), F32)
         return 0
@@ -163,26 +155,15 @@
             send_sem=z_ss.at[d, n, j], recv_sem=z_rs.at[d, n, j],
             device_id=dev(dz=hop if d == 0 else -hop), device_id_type=MESH)
 
-    def x_copy(j):
-        return pltpu.make_async_remote_copy(
-            src_ref=tx_x.at[j], dst_ref=rx_x.at[j], send_sem=x_ss.at[j], recv_sem=x_rs.at[j],
-            device_id=dev(dh=1), device_id_type=MESH)
-
-    def a_copy(j):
-        return pltpu.make_async_remote_copy(
-            src_ref=resp.at[j], dst_ref=r_in.at[z, y % 2, (y // 2) * 2 + xl],
-            send_sem=a_ss.at[j], recv_sem=a_rs.at[j],
-            device_id=exchange_peer(j), device_id_type=MESH)
+    def a_copy(n, j):
+        return pltpu.make_async_remote_copy(
+            src_ref=tx_a.at[j], dst_ref=rx_a.at[n, j],
+            send_sem=a_ss.at[n, j], recv_sem=a_rs.at[n, j],
+            device_id=exchange_peer(j, n), device_id_type=MESH)
 
     def origin(j):
         dy, dx = group(j)
         return ((y + 4 - dy) % 4 // 2) * 2 + (xl + dx) % 2
-
-    def a_arrival(j):
-        return pltpu.make_async_remote_copy(
-            src_ref=resp.at[0], dst_ref=r_in.at[z, core, origin(j)],
-            send_sem=a_ss.at[j], recv_sem=a_rs.at[j],
-            device_id=dev(dc=1), device_id_type=MESH)
 
     def g_copy(d, far, j):
         back = 0 if far <= 2 else 2
@@ -244,56 +225,48 @@
             tx_z[d, 3, j] = value.astype(BF16)
             z_copy(d, 3, j).start()
 
-    def x_step(j):
+    def exchange(j):
         value = part_for(j, z)
         for n in (2, 3):
             for d in range(2):
                 z_copy(d, n, j).wait_recv()
                 value = value + rx_z[d, n, j].astype(F32)
-        grid_f[j, z] = value
-        tx_x[j] = value.astype(BF16)
-        x_copy(j).start()
+        value = value.astype(BF16)
+        tx_a[j] = value
+        a_copy(1, j).start()
+        if j == 0:
+            @pl.when(crossed)
+            def _():
+                a_copy(0, 0).start()
+
+            @pl.when(jnp.logical_not(crossed))
+            def _():
+                rx_a[0, 0] = value
+        else:
+            a_copy(0, j).start()
 
     def respond(j):
-        if j == 0:
-            for cp in fa_copies:
-                cp.wait()
         zh, zl = z // 4, z % 4
         gy, gx = group(j)
-        slot = 2 * gy + gx
+        other = ((y + 4 - gy) % 4) * 2 + (xl + gx) % 2
+        w = jnp.where(second, small[zl * 2 + 1], small[zl * 2])
+        for b in range(B32):
+            w = jnp.where(lane % B32 == b, w + small[A8 + other * B32 + b], w)
         s2 = msq[zh]
-        x_copy(j).wait_recv()
-        f = grid_f[j, z] + rx_x[j].astype(F32)
-        fb_row = jnp.zeros((1, 128), F32)
-        for b in range(B32):
-            fb_row = jnp.where(lane % B32 == b, small[A8 + pair * B32 + b], fb_row)
-        w = jnp.where(second, fas[slot, pl.ds(zl * 2 + 1, 1), :], fas[slot, pl.ds(zl * 2, 1), :]) + fb_row
         t = s2 - w * w
         g = mdf[zh] * w
         inv = 1.0 / (t * t + g * g)
         re = s2 * t * inv
-        im = -s2 * g * inv
-        out = (re * f + im * (sign * pltpu.roll(f, 64, 1))).astype(BF16)
+        im = -s2 * g * inv * sign
         if j == 0:
             @pl.when(crossed)
             def _():
-                resp[j] = out
-                a_copy(j).start()
-
-            @pl.when(jnp.logical_not(crossed))
-            def _():
-                r_in[z, y % 2, (y // 2) * 2 + xl] = out
+                a_copy(0, 0).wait_recv()
         else:
-            resp[j] = out
-            a_copy(j).start()
-
-    def g_first(j):
-        if j == 0:
-            @pl.when(crossed)
-            def _():
-                a_arrival(0).wait_recv()
-        else:
-            a_arrival(j).wait_recv()
+            a_copy(0, j).wait_recv()
+        a_copy(1, j).wait_recv()
+        f = rx_a[0, j].astype(F32) + rx_a[1, j].astype(F32)
+        r_in[z, core, origin(j)] = (re * f + im * pltpu.roll(f, 64, 1)).astype(BF16)
         for far in (2, 1):
             for d in range(2):
                 g_copy(d, far, j).start()
@@ -342,18 +315,18 @@
 
         lax.fori_loop(0, 2, half, 0)
 
-    STAGES = (z_first, z_second, x_step, respond, g_first, g_second, g_last)
+    STAGES = (z_first, z_second, exchange, respond, g_second, g_last)
 
     def stage(j, k):
         STAGES[k](j)
+        if j == 3 and k == 4:
+            arrange(0)
         if j == 3 and k == 5:
-            arrange(0)
-        if j == 3 and k == 6:
             for dz in (1, -1, 2, -2):
                 arrange(dz)
 
-    WHEN = ((4, 6, 8, 9, 10, 11, 12), (6, 8, 9, 10, 11, 12, 13),
-            (8, 9, 10, 11, 12, 13, 14), (10, 11, 12, 13, 14, 15, 16))
+    WHEN = ((4, 6, 8, 9, 10, 11), (6, 8, 9, 10, 11, 12),
+            (8, 9, 10, 11, 12, 13), (10, 11, 12, 13, 14, 15))
 
     def events(t):
         return [(j, WHEN[j].index(t)) for j in (3, 2, 1, 0) if t in WHEN[j]]
@@ -464,7 +437,7 @@
 
     lax.fori_loop(0, 2, last_half, 0)
     send_sibling(3, 1)
-    for t in range(8, 17):
+    for t in range(8, 16):
         for j, k in events(t):
             stage(j, k)
     for dz in (3, -3, -4):
@@ -475,7 +448,6 @@
 
     def drain(j, _):
         sib_copy(j).wait_send()
-        x_copy(j).wait_send()
         return 0
 
     lax.fori_loop(0, 4, drain, 0)
@@ -485,11 +457,13 @@
                 if n != 1 or far_side(d, j):
                     z_copy(d, n, j).wait_send()
     for j in range(1, 4):
-        a_copy(j).wait_send()
+        a_copy(0, j).wait_send()
+    for j in range(4):
+        a_copy(1, j).wait_send()
 
     @pl.when(crossed)
     def _():
-        a_copy(0).wait_send()
+        a_copy(0, 0).wait_send()
 
     for j in range(4):
         for far in range(1, 5):
@@ -501,11 +475,20 @@
 
 
 def stress_kernel(ms, rhs, out, acc):
+    count = out.shape[0]
+    lhs = ms[...].T
     for ra in range(16):
         r = rhs[ra].reshape(2 * MH, 256)[:M]
-        acc[:, ra, :] = lax.dot_general(
-            ms[...], r, (((0,), (0,)), ((), ())), preferred_element_type=F32)
-    out[...] = acc[...].reshape(out.shape).astype(BF16)
+        acc[ra] = lax.dot_general(
+            lhs, r, (((1,), (0,)), ((), ())), preferred_element_type=F32).astype(BF16)
+    to = lax.broadcasted_iota(jnp.int32, (128, 128), 0)
+    of = lax.broadcasted_iota(jnp.int32, (128, 128), 1)
+    swap = jnp.where((to % 8 == of // 16) & (to // 8 == of % 16), 1.0, 0.0).astype(BF16)
+    for r_ in range(2):
+        for e in range(0, count, 16):
+            rows = jnp.concatenate([acc[r_ * 8 + a, e:e + 16, :] for a in range(A8)], 0)
+            turned = lax.dot_general(swap, rows, (((1,), (0,)), ((), ())), preferred_element_type=F32)
+            out[e:e + 16, r_] = turned.astype(BF16).reshape(16, A8, 256)
 
 
 def local(vel_a, vel_b, panel_modes, modal_stress, freq_a, freq_b, mode_freq, damping):
@@ -525,7 +508,6 @@
             pltpu.VMEM((M, KD), BF16),
             pltpu.VMEM((8, 2, 4, MH, 128), BF16),
             pltpu.VMEM((8, 48, KD), BF16),
-            pltpu.VMEM((8, A8, 128), F32),
             pltpu.VMEM((2, MH, 128), F32),
             pltpu.VMEM((2, MH, 128), F32),
             pltpu.VMEM((KT, 9, B32, 128), F32),
@@ -538,18 +520,17 @@
             pltpu.VMEM((2, 4, 4, MH, 128), BF16),
             pltpu.VMEM((2, 4, 4, MH, 128), BF16),
             pltpu.VMEM((4, MH, 128), BF16),
-            pltpu.VMEM((4, MH, 128), BF16),
-            pltpu.VMEM((4, MH, 128), BF16),
-            dma((9,)), dma((9,)), dma((7,)), dma((7,)), dma((4,)), dma((4,)),
-            dma((2, 4, 4)), dma((2, 4, 4)), dma((4,)), dma((4,)),
-            dma((4,)), dma((4,)), dma((2, 4, 4)), dma((2, 4, 4)), dma((8, 4)), dma((8, 4)),
+            pltpu.VMEM((2, 4, MH, 128), BF16),
+            dma((9,)), dma((9,)), dma((4,)), dma((4,)),
+            dma((2, 4, 4)), dma((2, 4, 4)),
+            dma((2, 4)), dma((2, 4)), dma((2, 4, 4)), dma((2, 4, 4)), dma((8, 4)), dma((8, 4)),
             dma((3,)),
         ],
         compiler_params=pltpu.CompilerParams(
             collective_id=0, has_side_effects=True, vmem_limit_bytes=48 * 1024 * 1024),
     )(va, vb, panel_modes, small)
     elements = modal_stress.shape[1]
-    tile = 128
+    tile = 256
     return pl.pallas_call(
         stress_kernel,
         out_shape=jax.ShapeDtypeStruct((elements, 2, A8, 256), BF16),
@@ -559,7 +540,7 @@
             pl.BlockSpec((16, 2, MH, 256), lambda i: (0, 0, 0, 0)),
         ],
         out_specs=pl.BlockSpec((tile, 2, A8, 256), lambda i: (i, 0, 0, 0)),
-        scratch_shapes=[pltpu.VMEM((tile, 16, 256), F32)],
+        scratch_shapes=[pltpu.VMEM((16, tile, 256), BF16)],
         compiler_params=pltpu.CompilerParams(vmem_limit_bytes=48 * 1024 * 1024),
     )(modal_stress, r)
 

time: 76 us -> 73.9 us (0.972)
  Pallas kernels: 71.8 us -> 69.6 us
    pallas_call x1, Pallas kernels: 5.8 us -> 3.94 us  [local(): pl.pallas_call(stress_kernel, out_shape=jax.ShapeDtypeStruct((elements, 2...]
where the time goes in v3:
time: 73.9 us; the launch traced here: 73.7 us
  Pallas kernels  69.6 us (94%)
  local copies, waits for them, and re-layouts  3.22 us (4%)
  other arithmetic  0.83 us (1%)
    pallas_call x1, Pallas kernels, local(): pl.pallas_call(main_kernel, out_shape=jax.ShapeDtypeStruct((16, 2, MH, 25...  65.6 us
    pallas_call x1, Pallas kernels, local(): pl.pallas_call(stress_kernel, out_shape=jax.ShapeDtypeStruct((elements, 2...  3.94 us

profile of v3, /device:TPU:1, one launch (start us, length us, event | category | flops | bytes accessed | tf_op | source)
XLA Modules:
  0.0 73.7 jit_solution(7505068177074738059)
XLA Ops:
  0.0 0.0 copy-start.1
  0.0 0.8 %pad_maximum_fusion.small_in = f32[664]{0:T(1024)S(1)} fusion(f32[200]{0:T(256)} %param.15, f32[200]{0:T(256)} %param.14, f32[256]{0:T(256)} %param.13, f32[8]{0:T(128)} %param.12), kind=kLoop, calls=%fused_computation | loop fusion | flops 1992 | bytes 5312 | tf_op jit(solution)/shard_map/concatenate | solution.py:497
  0.8 0.9 %copy.9 = bf16[3,2,8,1792]{3,2,1,0:T(8,128)(2,1)S(1)} copy(bf16[3,2,8,1792]{3,1,0,2:T(2,128)(2,1)} %bitcast.7) | data formatting | bytes 344064 | tf_op jit(solution)/shard_map/transpose | solution.py:495
  1.8 1.2 %copy.10 = bf16[3,2,32,1792]{3,2,1,0:T(8,128)(2,1)S(1)} copy(bf16[3,2,32,1792]{3,1,0,2:T(2,128)(2,1)} %bitcast.6) | data formatting | bytes 1376256 | tf_op jit(solution)/shard_map/transpose | solution.py:496
  3.0 0.0 copy-start
  3.0 1.1 %copy-done = bf16[200,1792]{1,0:T(8,128)(2,1)S(1)} copy-done((bf16[200,1792]{1,0:T(8,128)(2,1)S(1)}, bf16[200,1792]{1,0:T(8,128)(2,1)}, u32[]{:S(2)}) %copy-start) | copy-done | bytes 716824
  4.1 65.6 %shard_map.82.rhs = bf16[16,2,104,256]{3,2,1,0:T(8,128)(2,1)S(1)} custom-call(bf16[48,1792]{1,0:T(8,128)(2,1)S(1)} %bitcast.5, bf16[192,1792]{1,0:T(8,128)(2,1)S(1)} %bitcast.4, bf16[200,1792]{1,0:T(8,128)(2,1)S(1)} %copy-done, f32[664]{0:T(1024)S(1)} %pad_maximum_fusion.small_in), custom_call_target="tpu_custom_call" | custom-call | tf_op jit(solution)/shard_map/pallas_call | solution.py:501
  69.7 0.0 copy-done.1
  69.7 3.9 %shard_map.83 = bf16[512,2,8,256]{3,2,1,0:T(8,128)(2,1)} custom-call(bf16[200,512]{1,0:T(8,128)(2,1)S(1)} %copy-done.1, bf16[16,2,104,256]{3,2,1,0:T(8,128)(2,1)S(1)} %shard_map.82.rhs), custom_call_target="tpu_custom_call" | custom-call | tf_op jit(solution)/shard_map/pallas_call | solution.py:534
Async XLA Ops:
  0.0 69.7 %copy-start.1 = (bf16[200,512]{1,0:T(8,128)(2,1)S(1)}, bf16[200,512]{1,0:T(8,128)(2,1)}, u32[]{:S(2)}) copy-start(bf16[200,512]{1,0:T(8,128)(2,1)} %ms.1) | copy-start | bytes 614404
  3.0 1.1 %copy-start = (bf16[200,1792]{1,0:T(8,128)(2,1)S(1)}, bf16[200,1792]{1,0:T(8,128)(2,1)}, u32[]{:S(2)}) copy-start(bf16[200,1792]{1,0:T(8,128)(2,1)} %modes_in.1) | copy-start | bytes 2150404

commit v4 on v3

--- a/solution.py
+++ b/solution.py
@@ -25,7 +25,7 @@
 def main_kernel(
     va, vb, modes_in, small_in,
     rhs,
-    small, modes, r_in, vel, msq, mdf, vf, uf, prs0, prs1, grid_f,
+    small, modes, r_in, vel, msq, mdf, vf, uf, prs, grid_f,
     tx_sib, rx_sib, tx_z, rx_z, tx_a, rx_a,
     vel_ss, vel_rs, sib_ss, sib_rs, z_ss, z_rs,
     a_ss, a_rs, g_ss, g_rs, gs_ss, gs_rs, loc_sem,
@@ -110,13 +110,14 @@
             mdf[h, pl.ds(n, 1), :] = jnp.full((1, 128), 2.0 * small[FD + h * MH + n] * f, F32)
         return 0
 
-    lax.fori_loop(0, 96, mode_row, 0)
-    for n in range(96, 104):
-        f = small[FM + n]
-        msq[0, n:n + 1, :] = jnp.full((1, 128), f * f, F32)
-        mdf[0, n:n + 1, :] = jnp.full((1, 128), 2.0 * small[FD + n] * f, F32)
-    msq[1, 96:104, :] = jnp.ones((8, 128), F32)
-    mdf[1, 96:104, :] = jnp.ones((8, 128), F32)
+    def mode_rows():
+        lax.fori_loop(0, 96, mode_row, 0)
+        for n in range(96, 104):
+            f = small[FM + n]
+            msq[0, n:n + 1, :] = jnp.full((1, 128), f * f, F32)
+            mdf[0, n:n + 1, :] = jnp.full((1, 128), 2.0 * small[FD + n] * f, F32)
+        msq[1, 96:104, :] = jnp.ones((8, 128), F32)
+        mdf[1, 96:104, :] = jnp.ones((8, 128), F32)
 
     def prep(kt, _):
         lanes = pl.ds(pl.multiple_of(kt * 128, 128), 128)
@@ -325,8 +326,10 @@
             for dz in (1, -1, 2, -2):
                 arrange(dz)
 
-    WHEN = ((4, 6, 8, 9, 10, 11), (6, 8, 9, 10, 11, 12),
-            (8, 9, 10, 11, 12, 13), (10, 11, 12, 13, 14, 15))
+    WHEN = ((3, 7, 8, 9, 10, 11),
+            (5, 8, 9, 10, 11, 12),
+            (7, 8, 9, 10, 11, 12),
+            (8, 9, 10, 11, 12, 13))
 
     def events(t):
         return [(j, WHEN[j].index(t)) for j in (3, 2, 1, 0) if t in WHEN[j]]
@@ -365,7 +368,6 @@
 
     own_modes.wait()
     own_vel.wait()
-    bufs = (prs0, prs1)
 
     def double_block(j, _):
         slots = (j % 2 + 4 * (j // 2), 2 + 4 * (j % 2) + j // 2)
@@ -396,15 +398,12 @@
 
                 @pl.when(j == 2)
                 def _():
+                    mode_rows()
                     c_xym.wait_recv()
 
                 @pl.when(j == 3)
                 def _():
                     c_xyp.wait_recv()
-
-            @pl.when(j >= 1)
-            def _():
-                send_sibling(j - 1, dx)
 
             for jj in range(4):
                 for t in events(2 * jj + dx):
@@ -412,32 +411,25 @@
                     def _():
                         stage(*t)
 
-            if dx == 0:
-                dst = jnp.where(jnp.logical_and(mine(1), j >= 1), jnp.maximum(j - 1, 0), 4)
-            else:
-                dst = jnp.where(mine(0), j, 4)
-
             def half(h, _):
-                forces(bufs[1 - dx], h, dst)
                 for k in range(7):
-                    pressure(bufs[dx], slot, h * 7 + k, k)
+                    pressure(prs, slot, h * 7 + k, k)
                 return 0
 
             lax.fori_loop(0, 2, half, 0)
+            dst = jnp.where(mine(dx), j, 4)
+
+            def force_half(h, _):
+                forces(prs, h, dst)
+                return 0
+
+            lax.fori_loop(0, 2, force_half, 0)
+            send_sibling(j, dx)
         return 0
 
     lax.fori_loop(0, 4, double_block, 0)
 
-    send_sibling(3, 0)
-    last = jnp.where(mine(1), 3, 4)
-
-    def last_half(h, _):
-        forces(prs1, h, last)
-        return 0
-
-    lax.fori_loop(0, 2, last_half, 0)
-    send_sibling(3, 1)
-    for t in range(8, 16):
+    for t in range(8, 14):
         for j, k in events(t):
             stage(j, k)
     for dz in (3, -3, -4):
@@ -512,7 +504,6 @@
             pltpu.VMEM((2, MH, 128), F32),
             pltpu.VMEM((KT, 9, B32, 128), F32),
             pltpu.VMEM((7, 72, 128), F32),
-            pltpu.VMEM((512, KD), BF16),
             pltpu.VMEM((512, KD), BF16),
             pltpu.VMEM((5, 8, MH, 128), F32),
             pltpu.VMEM((4, 8, MH, 128), BF16),

time: 73.9 us -> 70.7 us (0.957)
  Pallas kernels: 69.6 us -> 66.5 us
    pallas_call x1, Pallas kernels: 65.6 us -> 62.5 us  [local(): pl.pallas_call(main_kernel, out_shape=jax.ShapeDtypeStruct((16, 2, MH, 25...]
where the time goes in v4:
time: 70.7 us; the launch traced here: 70.5 us
  Pallas kernels  66.5 us (94%)
  local copies, waits for them, and re-layouts  3.22 us (5%)
  other arithmetic  0.83 us (1%)
    pallas_call x1, Pallas kernels, local(): pl.pallas_call(main_kernel, out_shape=jax.ShapeDtypeStruct((16, 2, MH, 25...  62.5 us
    pallas_call x1, Pallas kernels, local(): pl.pallas_call(stress_kernel, out_shape=jax.ShapeDtypeStruct((elements, 2...  3.94 us

profile of v4, /device:TPU:1, one launch (start us, length us, event | category | flops | bytes accessed | tf_op | source)
XLA Modules:
  0.0 70.5 jit_solution(14948241236908500677)
XLA Ops:
  0.0 0.0 copy-start.1
  0.0 0.8 %pad_maximum_fusion.small_in = f32[664]{0:T(1024)S(1)} fusion(f32[200]{0:T(256)} %param.15, f32[200]{0:T(256)} %param.14, f32[256]{0:T(256)} %param.13, f32[8]{0:T(128)} %param.12), kind=kLoop, calls=%fused_computation | loop fusion | flops 1992 | bytes 5312 | tf_op jit(solution)/shard_map/concatenate | solution.py:489
  0.8 0.9 %copy.9 = bf16[3,2,8,1792]{3,2,1,0:T(8,128)(2,1)S(1)} copy(bf16[3,2,8,1792]{3,1,0,2:T(2,128)(2,1)} %bitcast.7) | data formatting | bytes 344064 | tf_op jit(solution)/shard_map/transpose | solution.py:487
  1.8 1.2 %copy.10 = bf16[3,2,32,1792]{3,2,1,0:T(8,128)(2,1)S(1)} copy(bf16[3,2,32,1792]{3,1,0,2:T(2,128)(2,1)} %bitcast.6) | data formatting | bytes 1376256 | tf_op jit(solution)/shard_map/transpose | solution.py:488
  3.0 0.0 copy-start
  3.0 1.1 %copy-done = bf16[200,1792]{1,0:T(8,128)(2,1)S(1)} copy-done((bf16[200,1792]{1,0:T(8,128)(2,1)S(1)}, bf16[200,1792]{1,0:T(8,128)(2,1)}, u32[]{:S(2)}) %copy-start) | copy-done | bytes 716824
  4.1 62.5 %shard_map.82.rhs = bf16[16,2,104,256]{3,2,1,0:T(8,128)(2,1)S(1)} custom-call(bf16[48,1792]{1,0:T(8,128)(2,1)S(1)} %bitcast.5, bf16[192,1792]{1,0:T(8,128)(2,1)S(1)} %bitcast.4, bf16[200,1792]{1,0:T(8,128)(2,1)S(1)} %copy-done, f32[664]{0:T(1024)S(1)} %pad_maximum_fusion.small_in), custom_call_target="tpu_custom_call" | custom-call | tf_op jit(solution)/shard_map/pallas_call | solution.py:493
  66.6 0.0 copy-done.1
  66.6 3.9 %shard_map.83 = bf16[512,2,8,256]{3,2,1,0:T(8,128)(2,1)} custom-call(bf16[200,512]{1,0:T(8,128)(2,1)S(1)} %copy-done.1, bf16[16,2,104,256]{3,2,1,0:T(8,128)(2,1)S(1)} %shard_map.82.rhs), custom_call_target="tpu_custom_call" | custom-call | tf_op jit(solution)/shard_map/pallas_call | solution.py:525
Async XLA Ops:
  0.0 66.6 %copy-start.1 = (bf16[200,512]{1,0:T(8,128)(2,1)S(1)}, bf16[200,512]{1,0:T(8,128)(2,1)}, u32[]{:S(2)}) copy-start(bf16[200,512]{1,0:T(8,128)(2,1)} %ms.1) | copy-start | bytes 614404
  3.0 1.1 %copy-start = (bf16[200,1792]{1,0:T(8,128)(2,1)S(1)}, bf16[200,1792]{1,0:T(8,128)(2,1)}, u32[]{:S(2)}) copy-start(bf16[200,1792]{1,0:T(8,128)(2,1)} %modes_in.1) | copy-start | bytes 2150404

commit v5 on v4

--- a/solution.py
+++ b/solution.py
@@ -332,7 +332,8 @@
             (8, 9, 10, 11, 12, 13))
 
     def events(t):
-        return [(j, WHEN[j].index(t)) for j in (3, 2, 1, 0) if t in WHEN[j]]
+        order = (0, 1, 2, 3) if t == 8 else (3, 2, 1, 0)
+        return [(j, WHEN[j].index(t)) for j in order if t in WHEN[j]]
 
     def forces(prs, h, dst):
         f = lax.dot_general(

time: 70.7 us -> 73.6 us (1.041)
  Pallas kernels: 66.5 us -> 69.3 us
    pallas_call x1, Pallas kernels: 62.5 us -> 65.4 us  [local(): pl.pallas_call(main_kernel, out_shape=jax.ShapeDtypeStruct((16, 2, MH, 25...]
where the time goes in v5:
time: 73.6 us; the launch traced here: 73.4 us
  Pallas kernels  69.3 us (94%)
  local copies, waits for them, and re-layouts  3.22 us (4%)
  other arithmetic  0.83 us (1%)
    pallas_call x1, Pallas kernels, local(): pl.pallas_call(main_kernel, out_shape=jax.ShapeDtypeStruct((16, 2, MH, 25...  65.4 us
    pallas_call x1, Pallas kernels, local(): pl.pallas_call(stress_kernel, out_shape=jax.ShapeDtypeStruct((elements, 2...  3.94 us

profile of v5, /device:TPU:1, one launch (start us, length us, event | category | flops | bytes accessed | tf_op | source)
XLA Modules:
  0.0 73.4 jit_solution(8033561043189351427)
XLA Ops:
  0.0 0.0 copy-start.1
  0.0 0.8 %pad_maximum_fusion.small_in = f32[664]{0:T(1024)S(1)} fusion(f32[200]{0:T(256)} %param.15, f32[200]{0:T(256)} %param.14, f32[256]{0:T(256)} %param.13, f32[8]{0:T(128)} %param.12), kind=kLoop, calls=%fused_computation | loop fusion | flops 1992 | bytes 5312 | tf_op jit(solution)/shard_map/concatenate | solution.py:490
  0.8 0.9 %copy.9 = bf16[3,2,8,1792]{3,2,1,0:T(8,128)(2,1)S(1)} copy(bf16[3,2,8,1792]{3,1,0,2:T(2,128)(2,1)} %bitcast.7) | data formatting | bytes 344064 | tf_op jit(solution)/shard_map/transpose | solution.py:488
  1.8 1.2 %copy.10 = bf16[3,2,32,1792]{3,2,1,0:T(8,128)(2,1)S(1)} copy(bf16[3,2,32,1792]{3,1,0,2:T(2,128)(2,1)} %bitcast.6) | data formatting | bytes 1376256 | tf_op jit(solution)/shard_map/transpose | solution.py:489
  3.0 0.0 copy-start
  3.0 1.1 %copy-done = bf16[200,1792]{1,0:T(8,128)(2,1)S(1)} copy-done((bf16[200,1792]{1,0:T(8,128)(2,1)S(1)}, bf16[200,1792]{1,0:T(8,128)(2,1)}, u32[]{:S(2)}) %copy-start) | copy-done | bytes 716824
  4.1 65.4 %shard_map.82.rhs = bf16[16,2,104,256]{3,2,1,0:T(8,128)(2,1)S(1)} custom-call(bf16[48,1792]{1,0:T(8,128)(2,1)S(1)} %bitcast.5, bf16[192,1792]{1,0:T(8,128)(2,1)S(1)} %bitcast.4, bf16[200,1792]{1,0:T(8,128)(2,1)S(1)} %copy-done, f32[664]{0:T(1024)S(1)} %pad_maximum_fusion.small_in), custom_call_target="tpu_custom_call" | custom-call | tf_op jit(solution)/shard_map/pallas_call | solution.py:494
  69.5 0.0 copy-done.1
  69.5 3.9 %shard_map.83 = bf16[512,2,8,256]{3,2,1,0:T(8,128)(2,1)} custom-call(bf16[200,512]{1,0:T(8,128)(2,1)S(1)} %copy-done.1, bf16[16,2,104,256]{3,2,1,0:T(8,128)(2,1)S(1)} %shard_map.82.rhs), custom_call_target="tpu_custom_call" | custom-call | tf_op jit(solution)/shard_map/pallas_call | solution.py:526
Async XLA Ops:
  0.0 69.5 %copy-start.1 = (bf16[200,512]{1,0:T(8,128)(2,1)S(1)}, bf16[200,512]{1,0:T(8,128)(2,1)}, u32[]{:S(2)}) copy-start(bf16[200,512]{1,0:T(8,128)(2,1)} %ms.1) | copy-start | bytes 614404
  3.0 1.1 %copy-start = (bf16[200,1792]{1,0:T(8,128)(2,1)S(1)}, bf16[200,1792]{1,0:T(8,128)(2,1)}, u32[]{:S(2)}) copy-start(bf16[200,1792]{1,0:T(8,128)(2,1)} %modes_in.1) | copy-start | bytes 2150404
